TPU v7x, 32 devices: a whole 2x2x4 slice. The times are simulated.
32 devices in a mesh: slab: 16 (over z, x, core), col: 2 (over y).
Axes of the slice: x: 2, y: 2, z: 4, core: 2. Of those that a mesh axis runs over, the one named last changes fastest.
Arguments:
- density: float32 [32, 64, 256], P('slab', 'col'), may hold values from 0.5 to 2
- velocity: float32 [3, 32, 64, 256], P(None, 'slab', 'col'), may hold values from -3 to 3
- pressure: float32 [32, 64, 256], P('slab', 'col'), may hold values from 0.5 to 2
- fraction_code: int32 [32, 64, 256], P('slab', 'col'), may hold values from 8 to 16
- interface_cell: int32 [16, 2, 512], P('slab', 'col'), may hold values from 0 to 16383
- interface_element: int32 [16, 2, 512], P('slab', 'col'), may hold values from 0 to 255
- interface_count: int32 [16, 2], P('slab', 'col'), may hold values from 64 to 512, as said below
- wall_normal: float32 [3, 16, 2, 512], P(None, 'slab', 'col'), may hold values from -4 to 4
- element_mass: float32 [16, 256], P('slab'), may hold values from 0.5 to 2
- element_removed: int32 [16, 256], P('slab'), may hold values 0 or 1
- element_velocity: float32 [3, 16, 256], P(None, 'slab'), may hold values from -3 to 3
Outputs:
- new_state: float32 [5, 32, 64, 256], P(None, 'slab', 'col')
- new_velocity: float32 [3, 16, 256], P(None, 'slab', 'col')
Inputs may be any that keep to these rules, and one draw needn't show every extreme that they name: `interface_cell`: index within the block of 2 x 32 x 256 cells of its slab and column. `interface_element`: element of the row's own slab group. `interface_count`: each count is 512, 256, 128 or 64; some slab and column has 512.
All inputs are finite; a program needn't handle non-finite values. No bound on the sum of `element_removed` on one device may be relied on, other than what follows from the above.
Results may differ from a plain program's by a relative error of at most 0.0003.
Values sent between devices are 32-bit elements; how exact they have to be, the bound alone decides.
A program may use at most 64 MiB of HBM per device.

v0:
```python
import functools

import jax
import jax.numpy as jnp
from jax import lax
from jax.experimental import pallas as pl
from jax.experimental.pallas import tpu as pltpu
from jax.sharding import PartitionSpec as P

ratio_heat = 1.4
step_ratio = 0.1
struct_step = 1.0
pieces = 2

MESH = pl.DeviceIdType.MESH
f32 = jnp.float32
bf16 = jnp.bfloat16


def conserved(rho, vel, p):
    u, v, w = vel
    energy = p * (1.0 / (ratio_heat - 1.0)) + 0.5 * rho * (u * u + v * v + w * w)
    return [rho, rho * u, rho * v, rho * w, energy]


def flux(state, vel, p, along):
    normal = vel[along]
    terms = [normal * q for q in state]
    terms[1 + along] = terms[1 + along] + p
    terms[4] = terms[4] + p * normal
    return terms


def sound(rho, p):
    return jnp.sqrt(ratio_heat * p / rho)


def face(low, high, along, keep=None):
    rho_l, vel_l, p_l, f_l, c_l = low
    rho_h, vel_h, p_h, f_h, c_h = high
    state_l, state_h = conserved(rho_l, vel_l, p_l), conserved(rho_h, vel_h, p_h)
    flux_l, flux_h = flux(state_l, vel_l, p_l, along), flux(state_h, vel_h, p_h, along)
    speed = jnp.maximum(jnp.abs(vel_l[along]) + c_l, jnp.abs(vel_h[along]) + c_h)
    aperture = 0.5 * jnp.minimum(f_l, f_h)
    if keep is not None:
        aperture = jnp.where(keep, aperture, 0.0)
    return [
        aperture * ((flux_l[k] + flux_h[k]) - speed * (state_h[k] - state_l[k]))
        for k in range(5)
    ]


def shifted(side, amount, axis):
    rho, vel, p, f, c = side
    move = lambda a: pltpu.roll(a, amount, axis)
    return (move(rho), [move(v) for v in vel], move(p), move(f), move(c))


def parts_of(value, count):
    found = []
    for _ in range(count):
        head = value.astype(bf16).astype(f32)
        found.append(head)
        value = value - head
    return found


def rows_of(rows, height):
    width = rows[0].shape[-1]
    at = lax.broadcasted_iota(jnp.int32, (height, width), 0)
    total = jnp.zeros((height, width), f32)
    for k, row in enumerate(rows):
        total = jnp.where(at == k, row, total)
    return total


def dot_nn(a, b):
    return lax.dot_general(a, b, (((1,), (0,)), ((), ())), preferred_element_type=f32)


def dot_nt(a, b):
    return lax.dot_general(a, b, (((1,), (1,)), ((), ())), preferred_element_type=f32)


def step_kernel(
    slabs,
    cols,
    rho_h,
    vel_h,
    p_h,
    code_h,
    cell_h,
    elem_h,
    count_h,
    normal_h,
    mass_h,
    removed_h,
    motion_h,
    out_h,
    new_h,
    rho_v,
    vel_v,
    p_v,
    code_v,
    cell_v,
    elem_v,
    count_v,
    normal_v,
    mass_v,
    removed_v,
    motion_v,
    halo_rho,
    halo_vel,
    halo_p,
    halo_code,
    edge_out,
    edge_in,
    loads,
    source,
    acc,
    new_full,
    new_own,
    local_sem,
    x_send,
    x_recv,
    y_send,
    y_recv,
    l_send,
    l_recv,
    out_sem,
    new_sem,
):
    bx, by, bz = rho_v.shape
    rows = cell_v.shape[-1]
    group = mass_v.shape[-1]
    share = group // cols
    s, c = lax.axis_index("slab"), lax.axis_index("col")
    has_down, has_up = s > 0, s < slabs - 1
    has_left, has_right = c > 0, c < cols - 1

    pairs = [
        (p_h, p_v),
        (code_h, code_v),
        (cell_h, cell_v),
        (rho_h, rho_v),
        (vel_h, vel_v),
        (normal_h, normal_v),
        (elem_h, elem_v),
        (count_h, count_v),
        (mass_h, mass_v),
        (removed_h, removed_v),
        (motion_h, motion_v),
    ]
    fetches = [
        pltpu.make_async_copy(src, dst, local_sem.at[i]) for i, (src, dst) in enumerate(pairs)
    ]
    for fetch in fetches:
        fetch.start()

    barrier = pltpu.get_barrier_semaphore()

    @pl.when(has_down)
    def _():
        pl.semaphore_signal(barrier, inc=1, device_id={"slab": s - 1}, device_id_type=MESH)

    @pl.when(has_up)
    def _():
        pl.semaphore_signal(barrier, inc=1, device_id={"slab": s + 1}, device_id_type=MESH)

    for step in range(1, cols):
        pl.semaphore_signal(
            barrier, inc=1, device_id={"col": lax.rem(c + step, cols)}, device_id_type=MESH
        )
    pl.semaphore_wait(
        barrier, has_down.astype(jnp.int32) + has_up.astype(jnp.int32) + (cols - 1)
    )

    tall = by // pieces

    def plane_copies(way, piece, peer):
        plane, slot, at = way * (bx - 1), 1 - way, pl.ds(piece * tall, tall)
        return [
            pltpu.make_async_remote_copy(
                src_ref=src,
                dst_ref=dst,
                send_sem=x_send.at[way, piece, i],
                recv_sem=x_recv.at[slot, piece, i],
                device_id={"slab": peer},
                device_id_type=MESH,
            )
            for i, (src, dst) in enumerate(
                [
                    (vel_h.at[:, plane, at], halo_vel.at[slot, :, at]),
                    (rho_h.at[plane, at], halo_rho.at[slot, at]),
                    (p_h.at[plane, at], halo_p.at[slot, at]),
                    (code_h.at[plane, at], halo_code.at[slot, at]),
                ]
            )
        ]

    def has_way(way):
        return jnp.logical_and(s - 1 + 2 * way >= 0, s - 1 + 2 * way < slabs)

    far = lax.rem(s, 2)
    for way in (far, 1 - far):

        @pl.when(has_way(way))
        def _():
            for piece in range(pieces):
                for copy in plane_copies(way, piece, s - 1 + 2 * way):
                    copy.start()

    def blank(slot):
        halo_rho[slot] = jnp.ones((by, bz), f32)
        halo_p[slot] = jnp.ones((by, bz), f32)
        halo_vel[slot] = jnp.zeros((3, by, bz), f32)
        halo_code[slot] = jnp.zeros((by, bz), jnp.int32)

    @pl.when(jnp.logical_not(has_down))
    def _():
        blank(0)

    @pl.when(jnp.logical_not(has_up))
    def _():
        blank(1)

    for fetch in fetches:
        fetch.wait()

    for side, y in ((0, 0), (1, by - 1)):
        for x in range(bx):
            edge_out[side, 0, x : x + 1, :] = rho_v[x, y : y + 1, :]
            for k in range(3):
                edge_out[side, 1 + k, x : x + 1, :] = vel_v[k, x, y : y + 1, :]
            edge_out[side, 4, x : x + 1, :] = p_v[x, y : y + 1, :]
            edge_out[side, 5, x : x + 1, :] = code_v[x, y : y + 1, :].astype(f32) * (1.0 / 16.0)

    def edge_copy(side, slot, peer):
        return pltpu.make_async_remote_copy(
            src_ref=edge_out.at[side],
            dst_ref=edge_in.at[slot],
            send_sem=y_send.at[slot],
            recv_sem=y_recv.at[slot],
            device_id={"col": peer},
            device_id_type=MESH,
        )

    @pl.when(has_left)
    def _():
        edge_copy(0, 1, c - 1).start()

    @pl.when(has_right)
    def _():
        edge_copy(1, 0, c + 1).start()

    cells = cell_v[0]
    line = lax.shift_right_logical(cells, bz.bit_length() - 1)
    place = lax.bitwise_and(cells, bz - 1)
    at_line = lax.broadcasted_iota(jnp.int32, (bx * by, rows), 0) == line
    at_place = (lax.broadcasted_iota(jnp.int32, (bz, rows), 0) == place).astype(f32).astype(bf16)
    at_elem = (
        (lax.broadcasted_iota(jnp.int32, (group, rows), 0) == elem_v[0]).astype(f32).astype(bf16)
    )
    active = (lax.broadcasted_iota(jnp.int32, (1, rows), 1) < count_v[...]).astype(f32)

    fraction = code_v[...].astype(f32) * (1.0 / 16.0)
    wetted = (p_v[...] * (1.0 - fraction)).reshape(bx * by, bz)
    picked = dot_nn(jnp.concatenate(parts_of(wetted, 3), axis=0).astype(bf16), at_place)
    size = bx * by
    picked = picked[:size] + picked[size : 2 * size] + picked[2 * size :]
    weight = jnp.sum(jnp.where(at_line, picked, 0.0), axis=0, keepdims=True) * active
    normals = [normal_v[k, 0] for k in range(3)]
    pushes = [weight * n for n in normals]

    force = rows_of([-q for q in pushes], 8)
    force = jnp.concatenate(parts_of(force, 3) + [jnp.zeros_like(force)], axis=0).astype(bf16)
    found = dot_nt(force, at_elem)
    loads[c] = found[0:8] + found[8:16] + found[16:24]

    def load_copy(step):
        return pltpu.make_async_remote_copy(
            src_ref=loads.at[c],
            dst_ref=loads.at[c],
            send_sem=l_send.at[step - 1],
            recv_sem=l_recv.at[step - 1],
            device_id={"col": lax.rem(c + step, cols)},
            device_id_type=MESH,
        )

    for step in range(1, cols):
        load_copy(step).start()

    def spread(values):
        total = None
        for part in zip(*[parts_of(v, 2) for v in values]):
            lhs = jnp.concatenate([jnp.where(at_line, q, 0.0) for q in part], axis=0)
            found = dot_nt(lhs.astype(bf16), at_place)
            total = found if total is None else total + found
        return total.reshape(len(values), bx, by, bz)

    source[0:3] = spread(pushes)

    high = 16

    def inner(i, carry):
        at = pl.ds(pl.multiple_of(i * high, high), high)
        lane = lax.broadcasted_iota(jnp.int32, (high, bz), 1) < bz - 1
        before, upper = None, None
        for x in range(bx):
            rho, p = rho_v[x, at, :], p_v[x, at, :]
            vel = [vel_v[k, x, at, :] for k in range(3)]
            side = (rho, vel, p, code_v[x, at, :].astype(f32) * (1.0 / 16.0), sound(rho, p))
            through = face(side, shifted(side, bz - 1, 1), 2, lane)
            total = [q - pltpu.roll(q, 1, 1) for q in through]
            if before is not None:
                across = face(before, side, 0)
                for k in range(5):
                    acc[k, x - 1, at, :] = upper[k] + across[k]
                total = [total[k] - across[k] for k in range(5)]
            before, upper = side, total
        for k in range(5):
            acc[k, bx - 1, at, :] = upper[k]
        return carry

    lax.fori_loop(0, by // high, inner, 0)

    halves = bz // 128

    def inner_y(i, carry):
        x = i // halves
        at = pl.ds(pl.multiple_of((i % halves) * 128, 128), 128)
        below = lax.broadcasted_iota(jnp.int32, (by, 128), 0) < by - 1
        rho, p = rho_v[x, :, at], p_v[x, :, at]
        vel = [vel_v[k, x, :, at] for k in range(3)]
        side = (rho, vel, p, code_v[x, :, at].astype(f32) * (1.0 / 16.0), sound(rho, p))
        through = face(side, shifted(side, by - 1, 0), 1, below)
        for k in range(5):
            acc[k, x, :, at] += through[k] - pltpu.roll(through[k], 1, 0)
        return carry

    lax.fori_loop(0, bx * halves, inner_y, 0)

    def packed(ref, slot):
        rho, p = ref[slot, 0], ref[slot, 4]
        return (rho, [ref[slot, 1 + k] for k in range(3)], p, ref[slot, 5], sound(rho, p))

    @pl.when(has_left)
    def _():
        edge_copy(1, 0, c - 1).wait_recv()
        through = face(packed(edge_in, 0), packed(edge_out, 0), 1)
        for k in range(5):
            for x in range(bx):
                acc[k, x, 0:1, :] -= through[k][x : x + 1]

    @pl.when(has_right)
    def _():
        edge_copy(0, 1, c + 1).wait_recv()
        through = face(packed(edge_out, 1), packed(edge_in, 1), 1)
        for k in range(5):
            for x in range(bx):
                acc[k, x, by - 1 : by, :] += through[k][x : x + 1]

    for step in range(1, cols):
        load_copy(step).wait_recv()
    total = loads[0]
    for other in range(1, cols):
        total = total + loads[other]
    keep = 1.0 - removed_v[...].astype(f32)
    start = rows_of([motion_v[k] for k in range(3)], 8)
    moved = (start + struct_step * total / mass_v[...]) * keep
    new_full[...] = moved
    own = new_full[:, pl.ds(pl.multiple_of(c * share, share), share)]
    for k in range(3):
        new_own[k] = own[k : k + 1]
    new_copy = pltpu.make_async_copy(new_own, new_h, new_sem)
    new_copy.start()
    moved = jnp.concatenate(parts_of(moved, 3) + [jnp.zeros_like(moved)], axis=0).astype(bf16)
    found = dot_nn(moved, at_elem)
    found = found[0:8] + found[8:16] + found[16:24]
    work = jnp.sum(rows_of(normals, 8) * found, axis=0, keepdims=True)
    source[3:4] = spread([weight * work])

    def join(i, carry):
        x = i // (by // high)
        at = pl.ds(pl.multiple_of((i % (by // high)) * high, high), high)
        rho, p = rho_v[x, at, :], p_v[x, at, :]
        state = conserved(rho, [vel_v[k, x, at, :] for k in range(3)], p)
        scale = step_ratio / (code_v[x, at, :].astype(f32) * (1.0 / 16.0))
        acc[0, x, at, :] = state[0] - scale * acc[0, x, at, :]
        for k in range(4):
            acc[1 + k, x, at, :] = state[1 + k] - scale * (
                acc[1 + k, x, at, :] - source[k, x, at, :]
            )
        return carry

    lax.fori_loop(0, bx * (by // high), join, 0)

    def out_copy(slot, piece):
        plane, at = slot * (bx - 1), pl.ds(piece * tall, tall)
        return pltpu.make_async_copy(
            acc.at[:, plane, at], out_h.at[:, plane, at], out_sem.at[slot, piece]
        )

    for slot in (1 - far, far):
        plane = slot * (bx - 1)
        sign = (1 - 2 * slot).astype(f32)

        for piece in range(pieces):

            @pl.when(has_way(slot))
            def _():
                for copy in plane_copies(1 - slot, piece, s - 1 + 2 * slot):
                    copy.wait_recv()

            def outer(i, carry):
                at = pl.ds(pl.multiple_of(piece * tall + i * high, high), high)
                rho, p = rho_v[plane, at, :], p_v[plane, at, :]
                vel = [vel_v[k, plane, at, :] for k in range(3)]
                own_fraction = code_v[plane, at, :].astype(f32) * (1.0 / 16.0)
                state = conserved(rho, vel, p)
                terms = flux(state, vel, p, 0)
                rho_n, p_n = halo_rho[slot, at, :], halo_p[slot, at, :]
                vel_n = [halo_vel[slot, k, at, :] for k in range(3)]
                fraction_n = halo_code[slot, at, :].astype(f32) * (1.0 / 16.0)
                state_n = conserved(rho_n, vel_n, p_n)
                terms_n = flux(state_n, vel_n, p_n, 0)
                speed = jnp.maximum(
                    jnp.abs(vel[0]) + sound(rho, p), jnp.abs(vel_n[0]) + sound(rho_n, p_n)
                )
                scale = (0.5 * step_ratio) * jnp.minimum(own_fraction, fraction_n) / own_fraction
                for k in range(5):
                    acc[k, plane, at, :] += scale * (
                        sign * (terms[k] + terms_n[k]) - speed * (state[k] - state_n[k])
                    )
                return carry

            lax.fori_loop(0, tall // high, outer, 0)
            out_copy(slot, piece).start()

    for slot in range(2):
        for piece in range(pieces):
            out_copy(slot, piece).wait()
    new_copy.wait()

    for way in range(2):

        @pl.when(has_way(way))
        def _():
            for piece in range(pieces):
                for copy in plane_copies(way, piece, s - 1 + 2 * way):
                    copy.wait_send()

    @pl.when(has_left)
    def _():
        edge_copy(0, 1, c - 1).wait_send()

    @pl.when(has_right)
    def _():
        edge_copy(1, 0, c + 1).wait_send()

    for step in range(1, cols):
        load_copy(step).wait_send()


def place_kernel(state, new, state_out, new_out, sem):
    copies = [
        pltpu.make_async_copy(state, state_out, sem.at[0]),
        pltpu.make_async_copy(new, new_out, sem.at[1]),
    ]
    for copy in copies:
        copy.start()
    for copy in copies:
        copy.wait()


def place(state, new):
    return pl.pallas_call(
        place_kernel,
        out_shape=tuple(jax.ShapeDtypeStruct(a.shape, a.dtype) for a in (state, new)),
        in_specs=[pl.BlockSpec(memory_space=pl.ANY)] * 2,
        out_specs=(pl.BlockSpec(memory_space=pl.ANY),) * 2,
        scratch_shapes=[pltpu.SemaphoreType.DMA((2,))],
        compiler_params=pltpu.CompilerParams(vmem_limit_bytes=4 * 1024 * 1024),
        name="place_results",
    )(state, new)


def local(slabs, cols, *args):
    density, velocity, pressure, code, cell, elem, count, normal, mass, removed, motion = args
    bx, by, bz = density.shape
    group = mass.shape[-1]
    share = group // cols
    plane = (by, bz)
    i32 = jnp.int32
    vmem, dma = pltpu.VMEM, pltpu.SemaphoreType.DMA
    args = [pltpu.with_memory_space_constraint(a, pltpu.HBM) if a.size > 1 else a for a in args]
    return place(*pl.pallas_call(
        functools.partial(step_kernel, slabs, cols),
        out_shape=(
            jax.ShapeDtypeStruct((5,) + density.shape, f32),
            jax.ShapeDtypeStruct((3, 1, share), f32),
        ),
        in_specs=[pl.BlockSpec(memory_space=pltpu.HBM)] * len(args),
        out_specs=(pl.BlockSpec(memory_space=pl.ANY), pl.BlockSpec(memory_space=pl.ANY)),
        scratch_shapes=[vmem(a.shape, a.dtype) for a in args]
        + [
            vmem((2,) + plane, f32),
            vmem((2, 3) + plane, f32),
            vmem((2,) + plane, f32),
            vmem((2,) + plane, i32),
            vmem((2, 6, bx, bz), f32),
            vmem((2, 6, bx, bz), f32),
            vmem((cols, 8, group), f32),
            vmem((4,) + density.shape, f32),
            vmem((5,) + density.shape, f32),
            vmem((8, group), f32),
            vmem((3, 1, share), f32),
            dma((len(args),)),
            dma((2, pieces, 4)),
            dma((2, pieces, 4)),
            dma((2,)),
            dma((2,)),
            dma((max(cols - 1, 1),)),
            dma((max(cols - 1, 1),)),
            dma((2, pieces)),
            dma,
        ],
        compiler_params=pltpu.CompilerParams(
            collective_id=0, has_side_effects=True, vmem_limit_bytes=16 * 1024 * 1024
        ),
        name="coupling_step",
    )(*args))


def solution(mesh):
    slabs, cols = mesh.shape["slab"], mesh.shape["col"]
    placed = (
        P("slab", "col", None),
        P(None, "slab", "col", None),
        P("slab", "col", None),
        P("slab", "col", None),
        P("slab", "col", None),
        P("slab", "col", None),
        P("slab", "col"),
        P(None, "slab", "col", None),
        P("slab", None),
        P("slab", None),
        P(None, "slab", None),
    )
    return jax.shard_map(
        functools.partial(local, slabs, cols),
        mesh=mesh,
        in_specs=placed,
        out_specs=(P(None, "slab", "col", None), P(None, "slab", "col")),
        check_vma=False,
    )
```

profile of v0, /device:TPU:9, one launch (start us, length us, event | category | flops | bytes accessed | tf_op | source)
XLA Modules:
  0.0 11.0 jit_solution(10707585363035227377)
XLA Ops:
  1.3 8.9 %coupling_step.1 = (f32[5,2,32,256]{3,2,1,0:T(8,128)S(1)}, f32[3,1,128]{2,1,0:T(1,128)S(1)}) custom-call(f32[2,32,256]{2,1,0:T(8,128)} %rho_h.1, f32[3,2,32,256]{3,2,1,0:T(8,128)} %vel_h.1, f32[2,32,256]{2,1,0:T(8,128)} %p_h.1, s32[2,32,256]{2,1,0:T(8,128)} %code_h.1, s32[1,1,512]{2,1,0:T(1,128)} %cell_h.1, s32[1,1,512]{2,1,0:T(1,128)} %elem_h.1, ...), custom_call_target="tpu_custom_call" | custom-call | tf_op jit(solution)/shard_map/coupling_step/pallas_call | solution.py:497
  10.2 0.7 %place_results.1 = (f32[5,2,32,256]{3,2,1,0:T(8,128)}, f32[3,1,128]{2,1,0:T(1,128)}) custom-call(f32[5,2,32,256]{3,2,1,0:T(8,128)S(1)} %get-tuple-element.4.state, f32[3,1,128]{2,1,0:T(1,128)S(1)} %get-tuple-element.5.new), custom_call_target="tpu_custom_call" | custom-call | tf_op jit(solution)/shard_map/place_results/pallas_call | solution.py:477
where the time goes:
time: 11.1 us; the launch traced here: 11 us
  Pallas kernels  9.69 us (87%)
  between operations  1.29 us (12%)
    pallas_call x1, Pallas kernels, local(): pl.pallas_call(functools.partial(step_kernel, slabs, cols), out_shape=(ja...  8.95 us
    pallas_call x1, Pallas kernels, place(): pl.pallas_call(place_kernel, out_shape=tuple((jax.ShapeDtypeStruct(a.shap...  0.75 us

commit v1 on v0

--- a/solution.py
+++ b/solution.py
@@ -154,9 +154,6 @@
     fetches = [
         pltpu.make_async_copy(src, dst, local_sem.at[i]) for i, (src, dst) in enumerate(pairs)
     ]
-    for fetch in fetches:
-        fetch.start()
-
     barrier = pltpu.get_barrier_semaphore()
 
     @pl.when(has_down)
@@ -171,6 +168,8 @@
         pl.semaphore_signal(
             barrier, inc=1, device_id={"col": lax.rem(c + step, cols)}, device_id_type=MESH
         )
+    for fetch in fetches:
+        fetch.start()
     pl.semaphore_wait(
         barrier, has_down.astype(jnp.int32) + has_up.astype(jnp.int32) + (cols - 1)
     )
@@ -201,14 +200,15 @@
     def has_way(way):
         return jnp.logical_and(s - 1 + 2 * way >= 0, s - 1 + 2 * way < slabs)
 
-    far = lax.rem(s, 2)
-    for way in (far, 1 - far):
-
+    def send_planes(way):
         @pl.when(has_way(way))
         def _():
             for piece in range(pieces):
                 for copy in plane_copies(way, piece, s - 1 + 2 * way):
                     copy.start()
+
+    far = lax.rem(s, 2)
+    send_planes(far)
 
     def blank(slot):
         halo_rho[slot] = jnp.ones((by, bz), f32)
@@ -289,6 +289,7 @@
 
     for step in range(1, cols):
         load_copy(step).start()
+    send_planes(1 - far)
 
     def spread(values):
         total = None

time: 11.1 us -> 11.1 us (level)
  no operation moved by 1% of the time
where the time goes in v1:
time: 11.1 us; the launch traced here: 11 us
  Pallas kernels  9.68 us (87%)
  between operations  1.29 us (12%)
    pallas_call x1, Pallas kernels, local(): pl.pallas_call(functools.partial(step_kernel, slabs, cols), out_shape=(ja...  8.94 us
    pallas_call x1, Pallas kernels, place(): pl.pallas_call(place_kernel, out_shape=tuple((jax.ShapeDtypeStruct(a.shap...  0.75 us

profile of v1, /device:TPU:9, one launch (start us, length us, event | category | flops | bytes accessed | tf_op | source)
XLA Modules:
  0.0 11.0 jit_solution(13780387440724120285)
XLA Ops:
  1.3 8.9 %coupling_step.1 = (f32[5,2,32,256]{3,2,1,0:T(8,128)S(1)}, f32[3,1,128]{2,1,0:T(1,128)S(1)}) custom-call(f32[2,32,256]{2,1,0:T(8,128)} %rho_h.1, f32[3,2,32,256]{3,2,1,0:T(8,128)} %vel_h.1, f32[2,32,256]{2,1,0:T(8,128)} %p_h.1, s32[2,32,256]{2,1,0:T(8,128)} %code_h.1, s32[1,1,512]{2,1,0:T(1,128)} %cell_h.1, s32[1,1,512]{2,1,0:T(1,128)} %elem_h.1, ...), custom_call_target="tpu_custom_call" | custom-call | tf_op jit(solution)/shard_map/coupling_step/pallas_call | solution.py:498
  10.2 0.7 %place_results.1 = (f32[5,2,32,256]{3,2,1,0:T(8,128)}, f32[3,1,128]{2,1,0:T(1,128)}) custom-call(f32[5,2,32,256]{3,2,1,0:T(8,128)S(1)} %get-tuple-element.4.state, f32[3,1,128]{2,1,0:T(1,128)S(1)} %get-tuple-element.5.new), custom_call_target="tpu_custom_call" | custom-call | tf_op jit(solution)/shard_map/place_results/pallas_call | solution.py:478

commit v2 on v1

--- a/solution.py
+++ b/solution.py
@@ -96,8 +96,8 @@
     mass_h,
     removed_h,
     motion_h,
-    out_h,
-    new_h,
+    acc,
+    new_own,
     rho_v,
     vel_v,
     p_v,
@@ -117,9 +117,7 @@
     edge_in,
     loads,
     source,
-    acc,
     new_full,
-    new_own,
     local_sem,
     x_send,
     x_recv,
@@ -127,8 +125,6 @@
     y_recv,
     l_send,
     l_recv,
-    out_sem,
-    new_sem,
 ):
     bx, by, bz = rho_v.shape
     rows = cell_v.shape[-1]
@@ -373,8 +369,6 @@
     own = new_full[:, pl.ds(pl.multiple_of(c * share, share), share)]
     for k in range(3):
         new_own[k] = own[k : k + 1]
-    new_copy = pltpu.make_async_copy(new_own, new_h, new_sem)
-    new_copy.start()
     moved = jnp.concatenate(parts_of(moved, 3) + [jnp.zeros_like(moved)], axis=0).astype(bf16)
     found = dot_nn(moved, at_elem)
     found = found[0:8] + found[8:16] + found[16:24]
@@ -395,12 +389,6 @@
         return carry
 
     lax.fori_loop(0, bx * (by // high), join, 0)
-
-    def out_copy(slot, piece):
-        plane, at = slot * (bx - 1), pl.ds(piece * tall, tall)
-        return pltpu.make_async_copy(
-            acc.at[:, plane, at], out_h.at[:, plane, at], out_sem.at[slot, piece]
-        )
 
     for slot in (1 - far, far):
         plane = slot * (bx - 1)
@@ -436,12 +424,6 @@
                 return carry
 
             lax.fori_loop(0, tall // high, outer, 0)
-            out_copy(slot, piece).start()
-
-    for slot in range(2):
-        for piece in range(pieces):
-            out_copy(slot, piece).wait()
-    new_copy.wait()
 
     for way in range(2):
 
@@ -502,7 +484,7 @@
             jax.ShapeDtypeStruct((3, 1, share), f32),
         ),
         in_specs=[pl.BlockSpec(memory_space=pltpu.HBM)] * len(args),
-        out_specs=(pl.BlockSpec(memory_space=pl.ANY), pl.BlockSpec(memory_space=pl.ANY)),
+        out_specs=(pl.BlockSpec(memory_space=pltpu.VMEM), pl.BlockSpec(memory_space=pltpu.VMEM)),
         scratch_shapes=[vmem(a.shape, a.dtype) for a in args]
         + [
             vmem((2,) + plane, f32),
@@ -513,9 +495,7 @@
             vmem((2, 6, bx, bz), f32),
             vmem((cols, 8, group), f32),
             vmem((4,) + density.shape, f32),
-            vmem((5,) + density.shape, f32),
             vmem((8, group), f32),
-            vmem((3, 1, share), f32),
             dma((len(args),)),
             dma((2, pieces, 4)),
             dma((2, pieces, 4)),
@@ -523,8 +503,6 @@
             dma((2,)),
             dma((max(cols - 1, 1),)),
             dma((max(cols - 1, 1),)),
-            dma((2, pieces)),
-            dma,
         ],
         compiler_params=pltpu.CompilerParams(
             collective_id=0, has_side_effects=True, vmem_limit_bytes=16 * 1024 * 1024

time: 11.1 us -> 11 us (level)
  no operation moved by 1% of the time
where the time goes in v2:
time: 11 us; the launch traced here: 10.9 us
  Pallas kernels  9.61 us (87%)
  between operations  1.29 us (12%)
    pallas_call x1, Pallas kernels, local(): pl.pallas_call(functools.partial(step_kernel, slabs, cols), out_shape=(ja...  8.86 us
    pallas_call x1, Pallas kernels, place(): pl.pallas_call(place_kernel, out_shape=tuple((jax.ShapeDtypeStruct(a.shap...  0.75 us

profile of v2, /device:TPU:9, one launch (start us, length us, event | category | flops | bytes accessed | tf_op | source)
XLA Modules:
  0.0 10.9 jit_solution(11304716183468414842)
XLA Ops:
  1.3 8.9 %coupling_step.1 = (f32[5,2,32,256]{3,2,1,0:T(8,128)S(1)}, f32[3,1,128]{2,1,0:T(1,128)S(1)}) custom-call(f32[2,32,256]{2,1,0:T(8,128)} %rho_h.1, f32[3,2,32,256]{3,2,1,0:T(8,128)} %vel_h.1, f32[2,32,256]{2,1,0:T(8,128)} %p_h.1, s32[2,32,256]{2,1,0:T(8,128)} %code_h.1, s32[1,1,512]{2,1,0:T(1,128)} %cell_h.1, s32[1,1,512]{2,1,0:T(1,128)} %elem_h.1, ...), custom_call_target="tpu_custom_call" | custom-call | tf_op jit(solution)/shard_map/coupling_step/pallas_call | solution.py:480
  10.1 0.7 %place_results.1 = (f32[5,2,32,256]{3,2,1,0:T(8,128)}, f32[3,1,128]{2,1,0:T(1,128)}) custom-call(f32[5,2,32,256]{3,2,1,0:T(8,128)S(1)} %get-tuple-element.4.state, f32[3,1,128]{2,1,0:T(1,128)S(1)} %get-tuple-element.5.new), custom_call_target="tpu_custom_call" | custom-call | tf_op jit(solution)/shard_map/place_results/pallas_call | solution.py:460
